TPU v7x, 32 devices: a whole 2x2x4 slice. The times are simulated.
32 devices in a mesh: row: 8 (over y, x, core), col: 4 (over z).
Axes of the slice: x: 2, y: 2, z: 4, core: 2. Of those that a mesh axis runs over, the one named last changes fastest.
Arguments:
- tokens: bfloat16 [8192, 5120], P('row'), may hold values from -6 to 6
- cotangent: bfloat16 [8192, 4096], P('row', 'col'), may hold values from -0.099609375 to 0.099609375
- small_weight: bfloat16 [2560, 4096], P(None, 'col'), may hold values from -0.125 to 0.125
- expand_in: bfloat16 [5120, 2560], P('row'), may hold values from -0.125 to 0.125
- expand_out: bfloat16 [4096, 4096], P('row', 'col'), may hold values from -0.09375 to 0.09375
Outputs:
- projected: bfloat16 [8192, 4096], P('row', 'col')
- grad_grown: float32 [5120, 4096], P('row', 'col')
- grad_in: float32 [5120, 2560], P('row', 'col')
- grad_out: float32 [4096, 4096], P('row', 'col')
All inputs are finite; a program needn't handle non-finite values.
Results may differ from a plain program's by a relative error of at most 0.014.
Values may be sent and summed in bfloat16 or wider, within the bound.
A program may use at most 128 MiB of HBM per device.

v0:
```python
import jax
import jax.numpy as jnp
from jax import lax
from jax.sharding import PartitionSpec as P


def body(tokens, cotangent, small_weight, expand_in, expand_out):
    mixed_part = jnp.dot(expand_in, small_weight, preferred_element_type=jnp.float32).astype(
        jnp.bfloat16
    )
    mixed_panel = lax.all_gather(mixed_part, "col", axis=1, tiled=True)
    out_panel = lax.all_gather(expand_out, "row", axis=0, tiled=True)
    grown = jnp.dot(mixed_panel, out_panel, preferred_element_type=jnp.float32).astype(jnp.bfloat16)
    columns = tokens
    projected = jnp.dot(
        columns,
        lax.all_gather(grown, "row", axis=0, tiled=True),
        preferred_element_type=jnp.float32,
    ).astype(jnp.bfloat16)
    columns = tokens
    grad_grown = lax.psum_scatter(
        lax.dot_general(
            columns, cotangent, (((0,), (0,)), ((), ())), preferred_element_type=jnp.float32
        ),
        "row",
        scatter_dimension=0,
        tiled=True,
    )
    grad_low = grad_grown.astype(jnp.bfloat16)
    back_part = lax.dot_general(
        grad_low, out_panel, (((1,), (1,)), ((), ())), preferred_element_type=jnp.float32
    )
    back = lax.psum_scatter(back_part, "col", scatter_dimension=1, tiled=True).astype(jnp.bfloat16)
    in_part = lax.dot_general(
        back, small_weight, (((1,), (1,)), ((), ())), preferred_element_type=jnp.float32
    )
    grad_in = lax.psum_scatter(
        in_part.astype(jnp.bfloat16), "col", scatter_dimension=1, tiled=True
    ).astype(jnp.float32)
    columns = mixed_panel
    grad_out = lax.psum_scatter(
        lax.dot_general(
            columns, grad_low, (((0,), (0,)), ((), ())), preferred_element_type=jnp.float32
        ).astype(jnp.bfloat16),
        "row",
        scatter_dimension=0,
        tiled=True,
    ).astype(jnp.float32)
    return (projected, grad_grown, grad_in, grad_out)


def solution(mesh):
    in_specs = (P("row", None), P("row", "col"), P(None, "col"), P("row", None), P("row", "col"))
    out_specs = (P("row", "col"), P("row", "col"), P("row", "col"), P("row", "col"))
    return jax.shard_map(body, mesh=mesh, in_specs=in_specs, out_specs=out_specs, check_vma=False)
```

profile of v0, /device:TPU:0, one launch (start us, length us, event | category | flops | bytes accessed | tf_op | source)
XLA Modules:
  0.0 703.5 jit_solution(6306562250412723693)
XLA Ops:
  7.2 0.7 all-gather.6.cloned.1.call-update
  8.0 18.5 %fusion.4 = f32[5120,1024]{1,0:T(8,128)} fusion(bf16[1024,5120]{1,0:T(8,128)(2,1)} %param.5, bf16[1024,1024]{1,0:T(8,128)(2,1)} %param.6), kind=kOutput, calls=%fused_computation.9 | convolution fusion | flops 10737418240 | bytes 33554432 | tf_op jit(solution)/shard_map/dot_general | solution.py:22
  26.5 0.0 all-gather.4.cloned.1.call-start
  26.5 7.1 %convolution_convert_fusion.2 = bf16[640,1024]{1,0:T(8,128)(2,1)} fusion(bf16[640,2560]{1,0:T(8,128)(2,1)S(1)} %copy-done, bf16[2560,1024]{1,0:T(8,128)(2,1)} %param.7), kind=kOutput, calls=%fused_computation.3 | convolution fusion | flops 3356098560 | bytes 9830400 | tf_op jit(solution)/shard_map/dot_general | solution.py:8
  33.7 33.3 %all-gather.6.cloned.1.call-done = bf16[4096,1024]{1,0:T(8,128)(2,1)} async-done(((bf16[512,1024]{1,0:T(8,128)(2,1)}), bf16[4096,1024]{1,0:T(8,128)(2,1)}) %all-gather.6.cloned.1.call-update) | async-done | bytes 8388624 | tf_op jit(solution)/shard_map/all_gather | solution.py:12
  67.0 140.2 %reduce-scatter.7.cloned.1.call-done = f32[640,1024]{1,0:T(8,128)} async-done(((f32[5120,1024]{1,0:T(8,128)}), f32[640,1024]{1,0:T(8,128)}) %reduce-scatter.7.cloned.1.call-update) | async-done | bytes 2621456 | tf_op jit(solution)/shard_map/reduce_scatter | solution.py:21
  207.2 11.9 %fusion.2 = f32[640,4096]{1,0:T(8,128)} fusion(bf16[4096,1024]{1,0:T(8,128)(2,1)} %all-gather.6.cloned.1.call-done, f32[640,1024]{1,0:T(8,128)} %reduce-scatter.7.cloned.1.call-done), kind=kOutput, calls=%fused_computation.7 | convolution fusion | flops 5369364480 | bytes 21495808 | tf_op jit(solution)/shard_map/dot_general | solution.py:30
  219.2 0.2 all-gather.8.cloned.1.call-start
  219.4 88.1 %all-gather.4.cloned.1.call-done = bf16[640,4096]{1,0:T(8,128)(2,1)} async-done(((bf16[640,1024]{1,0:T(8,128)(2,1)}), bf16[640,4096]{1,0:T(8,128)(2,1)}) %all-gather.4.cloned.1.call-update) | async-done | bytes 5242896 | tf_op jit(solution)/shard_map/all_gather | solution.py:11
  307.5 10.3 %convolution_convert_fusion.3 = bf16[640,1024]{1,0:T(8,128)(2,1)} fusion(bf16[640,4096]{1,0:T(8,128)(2,1)} %all-gather.4.cloned.1.call-done, bf16[4096,1024]{1,0:T(8,128)(2,1)} %all-gather.6.cloned.1.call-done), kind=kOutput, calls=%fused_computation.4 | convolution fusion | flops 5369364480 | bytes 14942208 | tf_op jit(solution)/shard_map/dot_general | solution.py:13
  317.8 0.0 reduce-scatter.11.cloned.1.call-start
  317.9 11.6 %convolution_convert_fusion = bf16[4096,1024]{1,0:T(8,128)(2,1)} fusion(bf16[640,4096]{1,0:T(8,128)(2,1)} %all-gather.4.cloned.1.call-done, f32[640,1024]{1,0:T(8,128)S(1)} %copy-done.2), kind=kOutput, calls=%fused_computation | convolution fusion | flops 5373558784 | bytes 16252928 | tf_op jit(solution)/shard_map/dot_general | solution.py:42
  329.5 0.0 reduce-scatter.13.cloned.1.call-start
  329.5 156.5 %reduce-scatter.9.cloned.1.call-done = f32[640,1024]{1,0:T(8,128)} async-done(((f32[640,4096]{1,0:T(8,128)}), f32[640,1024]{1,0:T(8,128)}) %reduce-scatter.9.cloned.1.call-update) | async-done | bytes 2621456 | tf_op jit(solution)/shard_map/reduce_scatter | solution.py:33
  486.0 6.9 convolution_convert_fusion.1
  492.9 3.4 copy.11
  496.4 56.3 %all-gather.8.cloned.1.call-done = bf16[5120,1024]{1,0:T(8,128)(2,1)} async-done(((bf16[640,1024]{1,0:T(8,128)(2,1)}), bf16[5120,1024]{1,0:T(8,128)(2,1)}) %all-gather.8.cloned.1.call-update) | async-done | bytes 10485776 | tf_op jit(solution)/shard_map/all_gather | solution.py:17
  552.7 17.9 %convert_bitcast_fusion = bf16[1024,1024]{0,1:T(8,128)(2,1)} fusion(bf16[5120,1024]{1,0:T(8,128)(2,1)} %all-gather.8.cloned.1.call-done, bf16[1024,5120]{1,0:T(8,128)(2,1)} %param.5), kind=kOutput, calls=%fused_computation.2 | convolution fusion | flops 10738466816 | bytes 23068672 | tf_op jit(solution)/shard_map/dot_general | solution.py:15
  570.6 4.1 copy.10
  574.7 52.7 %reduce-scatter.11.cloned.1.call-done = bf16[512,1024]{1,0:T(8,128)(2,1)} async-done(((bf16[4096,1024]{1,0:T(8,128)(2,1)}), bf16[512,1024]{1,0:T(8,128)(2,1)}) %reduce-scatter.11.cloned.1.call-update) | async-done | bytes 1048592 | tf_op jit(solution)/shard_map/reduce_scatter | solution.py:41
  627.3 2.8 convert_element_type.39
  630.1 62.0 %reduce-scatter.13.cloned.1.call-done = bf16[640,640]{1,0:T(8,128)(2,1)} async-done(((bf16[2560,640]{1,0:T(8,128)(2,1)}), bf16[640,640]{1,0:T(8,128)(2,1)}) %reduce-scatter.13.cloned.1.call-update) | async-done | bytes 819216
  692.1 2.2 copy.12
  694.3 2.4 convert_element_type.37
  (15 shorter events, 0.2 us)
Async XLA Ops:
  7.2 19.4 %copy-start = (bf16[640,2560]{1,0:T(8,128)(2,1)S(1)}, bf16[640,2560]{1,0:T(8,128)(2,1)}, u32[]{:S(2)}) copy-start(bf16[640,2560]{1,0:T(8,128)(2,1)} %param.8) | copy-start | bytes 9830404
  7.2 59.8 %all-gather.6.cloned.1.call-start = ((), (), s32[]{:S(2)}) async-start(), calls=%async_computation.5 | async-start | bytes 9437184 | tf_op jit(solution)/shard_map/all_gather | solution.py:12
  7.9 199.3 %reduce-scatter.7.cloned.1.call-start = ((), (), s32[]{:S(2)}) async-start(), calls=%async_computation.7 | async-start | bytes 23592960 | tf_op jit(solution)/shard_map/reduce_scatter | solution.py:21
  26.5 281.0 %all-gather.4.cloned.1.call-start = ((), (), s32[]{:S(2)}) async-start(), calls=%async_computation.4 | async-start | bytes 6553600 | tf_op jit(solution)/shard_map/all_gather | solution.py:11
  33.6 452.4 %reduce-scatter.9.cloned.1.call-start = ((), (), s32[]{:S(2)}) async-start(), calls=%async_computation.8 | async-start | bytes 13107200 | tf_op jit(solution)/shard_map/reduce_scatter | solution.py:33
  219.1 98.7 %copy-start.2 = (f32[640,1024]{1,0:T(8,128)S(1)}, f32[640,1024]{1,0:T(8,128)}, u32[]{:S(2)}) copy-start(f32[640,1024]{1,0:T(8,128)} %reduce-scatter.7.cloned.1.call-done) | copy-start | bytes 7864324
  219.2 333.5 %all-gather.8.cloned.1.call-start = ((), (), s32[]{:S(2)}) async-start(), calls=%async_computation.6 | async-start | bytes 11796480 | tf_op jit(solution)/shard_map/all_gather | solution.py:17
  317.8 309.5 %reduce-scatter.11.cloned.1.call-start = ((), (), s32[]{:S(2)}) async-start(), calls=%async_computation.9 | async-start | bytes 9437184 | tf_op jit(solution)/shard_map/reduce_scatter | solution.py:41
  329.5 362.6 %reduce-scatter.13.cloned.1.call-start = ((), (), s32[]{:S(2)}) async-start(), calls=%async_computation.10 | async-start | bytes 4096000
  552.7 144.0 %copy-start.1 = (bf16[640,2560]{1,0:T(8,128)(2,1)S(1)}, bf16[640,2560]{1,0:T(8,128)(2,1)}, u32[]{:S(2)}) copy-start(bf16[640,2560]{1,0:T(8,128)(2,1)} %param.8) | copy-start | bytes 9830404
Sparse Core Ops, SparseCore 0:
  9.9 57.0 all-gather.5
  71.2 135.9 reduce-scatter.6
  209.4 98.0 all-gather.3
  309.7 176.3 reduce-scatter.8
  488.3 64.3 all-gather.7
  556.0 71.2 reduce-scatter.10
  629.7 62.2 reduce-scatter.12
where the time goes:
time: 704 us
  waiting for transfers between devices  590 us (84%)
  matrix products  84.2 us (12%)
  between operations  14.2 us (2%)
  local copies, waits for them, and re-layouts  9.7 us (1%)
    reduce_scatter x1, waiting for transfers between devices, body(): lax.psum_scatter(back_part, 'col', scatter_dimension=1, tiled=True)  157 us
    reduce_scatter x1, waiting for transfers between devices, body(): lax.psum_scatter(lax.dot_general(columns, cotangent, (((0,), (0,)), ((),...  140 us
    all_gather x1, waiting for transfers between devices, body(): mixed_panel = lax.all_gather(mixed_part, 'col', axis=1, tiled=True)  88.1 us
    unnamed x8, waiting for transfers between devices  62.7 us
    all_gather x1, waiting for transfers between devices, body(): lax.all_gather(grown, 'row', axis=0, tiled=True)  56.3 us
    reduce_scatter x1, waiting for transfers between devices, body(): lax.psum_scatter(lax.dot_general(columns, grad_low, (((0,), (0,)), ((), (...  52.7 us
    all_gather x1, waiting for transfers between devices, body(): out_panel = lax.all_gather(expand_out, 'row', axis=0, tiled=True)  33.3 us
    dot_general x1, matrix products, body(): lax.dot_general(columns, cotangent, (((0,), (0,)), ((), ())), preferred_e...  18.5 us
  transfers between devices with their start and end apart: 7, of which 7 were waited for; matrix products, arithmetic and copies ran while one was open for 13% of the time, Pallas kernels for 0%

commit v1 on v0

v1 whole, which is shorter than its diff:
```python
import jax
import jax.numpy as jnp
from jax import lax
from jax.sharding import PartitionSpec as P

BF = jnp.bfloat16
F32 = jnp.float32


def dot(a, b, ca, cb):
    return lax.dot_general(a, b, (((ca,), (cb,)), ((), ())), preferred_element_type=F32)


def body(tokens, cotangent, small_weight, expand_in, expand_out):
    rows = lax.axis_size("row")
    r = lax.axis_index("row")
    band = small_weight.shape[0] // rows
    mine = lax.dynamic_slice_in_dim(small_weight, r * band, band, 0)
    small_rows = lax.all_gather(mine, "col", axis=1, tiled=True)
    out_panel = lax.all_gather(expand_out, "row", axis=0, tiled=True)
    grad_part = dot(tokens, cotangent, 0, 0).astype(BF)
    grad_sum = lax.psum_scatter(grad_part, "row", scatter_dimension=0, tiled=True)
    grad_grown = grad_sum.astype(F32)
    grad_low = grad_sum
    pair_part = dot(small_rows, out_panel, 1, 0).astype(BF)
    pair = lax.all_gather(pair_part, "row", axis=0, tiled=True)
    grown = dot(expand_in, pair, 1, 0).astype(BF)
    grown_all = lax.all_gather(grown, "row", axis=0, tiled=True)
    low_part = dot(expand_in, grad_low, 0, 0).astype(BF)
    low = lax.psum_scatter(low_part, "row", scatter_dimension=0, tiled=True)
    grad_in = lax.psum_scatter(
        dot(grad_low, pair, 1, 1).astype(BF), "col", scatter_dimension=1, tiled=True
    ).astype(F32)
    grad_out = lax.psum_scatter(
        dot(small_rows, low, 0, 0).astype(BF), "row", scatter_dimension=0, tiled=True
    ).astype(F32)
    projected = dot(tokens, grown_all, 1, 0).astype(BF)
    return (projected, grad_grown, grad_in, grad_out)


def solution(mesh):
    in_specs = (P("row", None), P("row", "col"), P(None, "col"), P("row", None), P("row", "col"))
    out_specs = (P("row", "col"), P("row", "col"), P("row", "col"), P("row", "col"))
    return jax.shard_map(body, mesh=mesh, in_specs=in_specs, out_specs=out_specs, check_vma=False)
```

time: 704 us -> 546 us (0.78)
  waiting for transfers between devices: 590 us -> 424 us
  local copies, waits for them, and re-layouts: 9.7 us -> 22.1 us
  matrix products: 84.2 us -> 75.6 us
    reduce_scatter x3 -> x2, waiting for transfers between devices: 349 us -> 148 us  [the longest x1 77 us: body(): lax.psum_scatter(grad_part, 'row', scatter_dimension=0, tiled=True)]
    unnamed x8 -> x10, waiting for transfers between devices: 62.7 us -> 90 us
    all_gather x1, waiting for transfers between devices: 33.3 us -> 55.1 us  [body(): out_panel = lax.all_gather(expand_out, 'row', axis=0, tiled=True)]
    all_gather x2 -> x3, waiting for transfers between devices: 144 us -> 131 us  [the longest x1 62.8 us: body(): grown_all = lax.all_gather(grown, 'row', axis=0, tiled=True)]
    unnamed x9 -> x6, local copies, waits for them, and re-layouts: 9.7 us -> 19.9 us
    dot_general x7, matrix products: 84.2 us -> 75.6 us  [dot(): lax.dot_general(a, b, (((ca,), (cb,)), ((), ())), preferred_element_type=...]
  transfers between devices with their start and end apart: 7 -> 8, of which waited for: 7 -> 8; matrix products, arithmetic and copies ran while one was open for 13% -> 15% of each run, Pallas kernels for 0% -> 0%
where the time goes in v1:
time: 546 us; the launch traced here: 545 us
  waiting for transfers between devices  424 us (78%)
  matrix products  75.6 us (14%)
  local copies, waits for them, and re-layouts  22.1 us (4%)
  between operations  14.2 us (3%)
  other arithmetic  8.34 us (2%)
    unnamed x10, waiting for transfers between devices  90 us
    reduce_scatter x1, waiting for transfers between devices, body(): lax.psum_scatter(grad_part, 'row', scatter_dimension=0, tiled=True)  77 us
    dot_general x7, matrix products, dot(): lax.dot_general(a, b, (((ca,), (cb,)), ((), ())), preferred_element_type=...  75.6 us
    reduce_scatter x1, waiting for transfers between devices, body(): lax.psum_scatter(dot(small_rows, low, 0, 0).astype(BF), 'row', scatter_di...  70.7 us
    all_gather x1, waiting for transfers between devices, body(): grown_all = lax.all_gather(grown, 'row', axis=0, tiled=True)  62.8 us
    all_gather x1, waiting for transfers between devices, body(): out_panel = lax.all_gather(expand_out, 'row', axis=0, tiled=True)  55.1 us
    all_gather x1, waiting for transfers between devices, body(): small_rows = lax.all_gather(mine, 'col', axis=1, tiled=True)  40.6 us
    all_gather x1, waiting for transfers between devices, body(): pair = lax.all_gather(pair_part, 'row', axis=0, tiled=True)  27.8 us
  transfers between devices with their start and end apart: 8, of which 8 were waited for; matrix products, arithmetic and copies ran while one was open for 15% of the time, Pallas kernels for 0%

profile of v1, /device:TPU:0, one launch (start us, length us, event | category | flops | bytes accessed | tf_op | source)
XLA Modules:
  0.0 544.9 jit_solution(578516714743725727)
XLA Ops:
  7.2 2.1 constant_dynamic-slice_fusion
  9.4 0.7 all-gather.7.cloned.1.call-update
  10.2 16.8 %convolution_convert_fusion = bf16[5120,1024]{1,0:T(8,128)(2,1)} fusion(bf16[1024,5120]{1,0:T(8,128)(2,1)} %param.5, bf16[1024,1024]{1,0:T(8,128)(2,1)} %param.6), kind=kOutput, calls=%fused_computation | convolution fusion | flops 10742661120 | bytes 23068672 | tf_op jit(solution)/shard_map/dot_general | solution.py:11
  27.1 40.6 %all-gather.5.cloned.1.call-done = bf16[320,4096]{1,0:T(8,128)(2,1)} async-done(((bf16[320,1024]{1,0:T(8,128)(2,1)}), bf16[320,4096]{1,0:T(8,128)(2,1)}) %all-gather.5.cloned.1.call-update) | async-done | bytes 2621456 | tf_op jit(solution)/shard_map/all_gather | solution.py:19
  67.7 55.1 %all-gather.7.cloned.1.call-done = bf16[4096,1024]{1,0:T(8,128)(2,1)} async-done(((bf16[512,1024]{1,0:T(8,128)(2,1)}), bf16[4096,1024]{1,0:T(8,128)(2,1)}) %all-gather.7.cloned.1.call-update) | async-done | bytes 8388624 | tf_op jit(solution)/shard_map/all_gather | solution.py:20
  122.8 8.0 %convolution_convert_fusion.5 = bf16[320,1024]{1,0:T(8,128)(2,1)} fusion(bf16[320,4096]{1,0:T(8,128)(2,1)} %all-gather.5.cloned.1.call-done, bf16[4096,1024]{1,0:T(8,128)(2,1)} %all-gather.7.cloned.1.call-done), kind=kOutput, calls=%fused_computation.8 | convolution fusion | flops 2684682240 | bytes 11665408 | tf_op jit(solution)/shard_map/dot_general | solution.py:11
  130.9 77.0 %reduce-scatter.9.cloned.1.call-done = bf16[640,1024]{1,0:T(8,128)(2,1)} async-done(((bf16[5120,1024]{1,0:T(8,128)(2,1)}), bf16[640,1024]{1,0:T(8,128)(2,1)}) %reduce-scatter.9.cloned.1.call-update) | async-done | bytes 1310736 | tf_op jit(solution)/shard_map/reduce_scatter | solution.py:22
  207.9 7.4 %fusion = bf16[2560,1024]{0,1:T(8,128)(2,1)} fusion(bf16[640,1024]{1,0:T(8,128)(2,1)} %reduce-scatter.9.cloned.1.call-done, bf16[640,2560]{1,0:T(8,128)(2,1)S(1)} %copy-done), kind=kOutput, calls=%fused_computation.3 | convolution fusion | flops 3358064640 | bytes 9830400 | tf_op jit(solution)/shard_map/dot_general | solution.py:11
  215.3 8.0 %copy.13 = bf16[2560,1024]{1,0:T(8,128)(2,1)} copy(bf16[2560,1024]{0,1:T(8,128)(2,1)} %fusion) | data formatting | bytes 10485760
  223.5 27.8 %all-gather.9.cloned.1.call-done = bf16[2560,1024]{1,0:T(8,128)(2,1)} async-done(((bf16[320,1024]{1,0:T(8,128)(2,1)}), bf16[2560,1024]{1,0:T(8,128)(2,1)}) %all-gather.9.cloned.1.call-update) | async-done | bytes 5242896 | tf_op jit(solution)/shard_map/all_gather | solution.py:26
  251.3 8.2 %convolution_convert_fusion.3 = bf16[640,2560]{1,0:T(8,128)(2,1)} fusion(bf16[640,1024]{1,0:T(8,128)(2,1)} %reduce-scatter.9.cloned.1.call-done, bf16[2560,1024]{1,0:T(8,128)(2,1)} %all-gather.9.cloned.1.call-done), kind=kOutput, calls=%fused_computation.4 | convolution fusion | flops 3357081600 | bytes 9830400 | tf_op jit(solution)/shard_map/dot_general | solution.py:11
  259.5 5.8 %copy.11 = bf16[640,2560]{0,1:T(8,128)(2,1)} copy(bf16[640,2560]{1,0:T(8,128)(2,1)} %convolution_convert_fusion.3) | data formatting | bytes 6553600
  265.4 45.7 %reduce-scatter.15.cloned.1.call-done = bf16[320,1024]{1,0:T(8,128)(2,1)} async-done(((bf16[2560,1024]{1,0:T(8,128)(2,1)}), bf16[320,1024]{1,0:T(8,128)(2,1)}) %reduce-scatter.15.cloned.1.call-update) | async-done | bytes 655376
  311.2 9.9 %convolution_convert_fusion.1 = bf16[4096,1024]{1,0:T(8,128)(2,1)} fusion(bf16[320,4096]{1,0:T(8,128)(2,1)} %all-gather.5.cloned.1.call-done, bf16[320,1024]{1,0:T(8,128)(2,1)} %reduce-scatter.15.cloned.1.call-done), kind=kOutput, calls=%fused_computation.1 | convolution fusion | flops 2688548864 | bytes 11665408 | tf_op jit(solution)/shard_map/dot_general | solution.py:11
  321.3 7.8 %fusion.1 = bf16[640,1024]{0,1:T(8,128)(2,1)} fusion(bf16[2560,1024]{1,0:T(8,128)(2,1)} %all-gather.9.cloned.1.call-done, bf16[640,2560]{1,0:T(8,128)(2,1)S(1)} %copy-done), kind=kOutput, calls=%fused_computation.7 | convolution fusion | flops 3356098560 | bytes 9830400 | tf_op jit(solution)/shard_map/dot_general | solution.py:11
  329.1 3.1 convert_element_type.45
  332.3 43.5 %reduce-scatter.13.cloned.1.call-done = bf16[640,640]{1,0:T(8,128)(2,1)} async-done(((bf16[2560,640]{1,0:T(8,128)(2,1)}), bf16[640,640]{1,0:T(8,128)(2,1)}) %reduce-scatter.13.cloned.1.call-update) | async-done | bytes 819216
  375.8 2.2 copy.12
  377.9 2.4 convert_element_type.47
  380.4 70.7 %reduce-scatter.11.cloned.1.call-done = bf16[512,1024]{1,0:T(8,128)(2,1)} async-done(((bf16[4096,1024]{1,0:T(8,128)(2,1)}), bf16[512,1024]{1,0:T(8,128)(2,1)}) %reduce-scatter.11.cloned.1.call-update) | async-done | bytes 1048592 | tf_op jit(solution)/shard_map/reduce_scatter | solution.py:34
  451.1 2.8 convert_element_type.51
  453.8 62.8 %all-gather.11.cloned.1.call-done = bf16[5120,1024]{0,1:T(8,128)(2,1)} async-done(((bf16[640,1024]{0,1:T(8,128)(2,1)}), bf16[5120,1024]{0,1:T(8,128)(2,1)}) %all-gather.11.cloned.1.call-update) | async-done | bytes 10485776 | tf_op jit(solution)/shard_map/all_gather | solution.py:28
  516.7 17.4 %convert_bitcast_fusion = bf16[1024,1024]{0,1:T(8,128)(2,1)} fusion(bf16[5120,1024]{0,1:T(8,128)(2,1)} %all-gather.11.cloned.1.call-done, bf16[1024,5120]{1,0:T(8,128)(2,1)} %param.5), kind=kOutput, calls=%fused_computation.5 | convolution fusion | flops 10738466816 | bytes 23068672 | tf_op jit(solution)/shard_map/dot_general | solution.py:11
  534.1 3.9 copy.10
  (17 shorter events, 0.9 us)
Async XLA Ops:
  7.2 200.7 %copy-start = (bf16[640,2560]{1,0:T(8,128)(2,1)S(1)}, bf16[640,2560]{1,0:T(8,128)(2,1)}, u32[]{:S(2)}) copy-start(bf16[640,2560]{1,0:T(8,128)(2,1)} %param.8) | copy-start | bytes 9830404
  7.2 60.5 %all-gather.5.cloned.1.call-start = ((), (), s32[]{:S(2)}) async-start(), calls=%async_computation.4 | async-start | bytes 3276800 | tf_op jit(solution)/shard_map/all_gather | solution.py:19
  9.4 113.4 %all-gather.7.cloned.1.call-start = ((), (), s32[]{:S(2)}) async-start(), calls=%async_computation.5 | async-start | bytes 9437184 | tf_op jit(solution)/shard_map/all_gather | solution.py:20
  10.1 197.7 %reduce-scatter.9.cloned.1.call-start = ((), (), s32[]{:S(2)}) async-start(), calls=%async_computation.8 | async-start | bytes 11796480 | tf_op jit(solution)/shard_map/reduce_scatter | solution.py:22
  27.0 224.3 %all-gather.9.cloned.1.call-start = ((), (), s32[]{:S(2)}) async-start(), calls=%async_computation.6 | async-start | bytes 5898240 | tf_op jit(solution)/shard_map/all_gather | solution.py:26
  130.8 180.4 %reduce-scatter.15.cloned.1.call-start = ((), (), s32[]{:S(2)}) async-start(), calls=%async_computation.11 | async-start | bytes 5898240
  223.3 152.5 %reduce-scatter.13.cloned.1.call-start = ((), (), s32[]{:S(2)}) async-start(), calls=%async_computation.10 | async-start | bytes 4096000
  265.4 185.7 %reduce-scatter.11.cloned.1.call-start = ((), (), s32[]{:S(2)}) async-start(), calls=%async_computation.9 | async-start | bytes 9437184 | tf_op jit(solution)/shard_map/reduce_scatter | solution.py:34
  321.0 195.6 %all-gather.11.cloned.1.call-start = ((), (), s32[]{:S(2)}) async-start(), calls=%async_computation.7 | async-start | bytes 11796480 | tf_op jit(solution)/shard_map/all_gather | solution.py:28
Sparse Core Ops, SparseCore 0:
  10.2 57.4 all-gather.4
  69.5 53.1 all-gather.6
  126.3 81.5 reduce-scatter.8
  210.2 41.0 all-gather.8
  254.5 56.5 reduce-scatter.14
  313.4 62.2 reduce-scatter.12
  379.6 71.3 reduce-scatter.10
  453.5 63.0 all-gather.10

commit v2 on v1

v2 whole, which is shorter than its diff:
```python
import functools

import jax
import jax.numpy as jnp
from jax import lax
from jax.experimental import pallas as pl
from jax.experimental.pallas import tpu as pltpu
from jax.sharding import PartitionSpec as P

BF = jnp.bfloat16
F32 = jnp.float32
TILE = 16
CHUNKS = 2


def dot(a, b, ca, cb):
    return lax.dot_general(a, b, (((ca,), (cb,)), ((), ())), preferred_element_type=F32)


def exchange_kernel(rows, gathers, scatters, *refs):
    na, nr = len(gathers), len(scatters)
    ag_in, rs_in = refs[:na], refs[na : na + nr]
    ag_out, rs_out = refs[na + nr : 2 * na + nr], refs[2 * na + nr : 2 * na + 2 * nr]
    scratch = refs[2 * na + 2 * nr :]
    bufs = [scratch[6 * i : 6 * i + 6] for i in range(nr)]
    send_sems, recv_sems, local_sems = scratch[6 * nr :]
    span = rows // 4
    r = lax.axis_index("row")
    core, b, a = r % 2, (r // 2) % 2, r // 4

    def index(j, db, dk):
        return ((a + j) % span * 2 + (b + db) % 2) * 2 + (core + dk) % 2

    sib, side = index(0, 0, 1), index(0, 1, 0)
    along = [index(j, 0, 0) for j in range(1, span)]
    behind = [index(span - j, 0, 0) for j in range(1, span)]
    corner = [index(span - j, 1, 0) for j in range(1, span)]

    barrier = pltpu.get_barrier_semaphore()
    for peer in [sib, side] + along:
        pl.semaphore_signal(
            barrier, inc=1, device_id={"row": peer}, device_id_type=pl.DeviceIdType.MESH
        )
    pl.semaphore_wait(barrier, span + 1)

    copies = []

    def push(src, dst, peer):
        i = len(copies)
        copy = pltpu.make_async_remote_copy(
            src_ref=src,
            dst_ref=dst,
            send_sem=send_sems.at[i],
            recv_sem=recv_sems.at[i],
            device_id={"row": peer},
            device_id_type=pl.DeviceIdType.MESH,
        )
        copy.start()
        copies.append(copy)
        return copy

    def at(block, n, start, size):
        return pl.ds(pl.multiple_of(block * n + start, 16), size)

    parts = []
    for i, (_, w) in enumerate(scatters):
        for c in range(CHUNKS):
            parts.append((i, pl.ds(c * (w // CHUNKS), w // CHUNKS)))

    first = []
    for i, cols in parts:
        n = scatters[i][0] // rows
        first.append(
            [
                push(
                    rs_in[i].at[at(index(q // 2, q % 2, 1), n, 0, n), cols],
                    bufs[i][0].at[q, :, cols],
                    sib,
                )
                for q in list(range(1, 2 * span)) + [0]
            ]
        )

    locals_ = []
    own = []
    for i, (n, _) in enumerate(gathers):
        h = n // 2
        x, o = ag_in[i], ag_out[i]
        copy = pltpu.make_async_copy(x, o.at[at(r, n, 0, n)], local_sems.at[i])
        copy.start()
        locals_.append(copy)
        b1 = push(x.at[pl.ds(0, h)], o.at[at(r, n, 0, h)], side)
        a2 = [push(x.at[pl.ds(h, h)], o.at[at(r, n, h, h)], p) for p in along]
        b2 = push(x.at[pl.ds(h, h)], o.at[at(r, n, h, h)], side)
        a1 = [push(x.at[pl.ds(0, h)], o.at[at(r, n, 0, h)], p) for p in along]
        s = push(x, o.at[at(r, n, 0, n)], sib)
        own.append((b1, a2, b2, a1, s))

    def add(size, store, *loads):
        def step(t):
            sl = pl.ds(pl.multiple_of(t * TILE, TILE), TILE)
            total = loads[0](sl).astype(F32)
            for load in loads[1:]:
                total = total + load(sl).astype(F32)
            store(sl, total)

        pl.loop(0, size // TILE)(step)

    def shift(sl, start):
        return pl.ds(pl.multiple_of(sl.start + start, TILE), TILE)

    hop1 = []
    for (i, cols), arrivals in zip(parts, first):
        n = scatters[i][0] // rows
        h = n // 2
        x = rs_in[i]
        sibs, acc, r1b, r1a, _, _ = bufs[i]
        for copy in arrivals:
            copy.wait_recv()
        for q in range(1, 2 * span):
            base = index(q // 2, q % 2, 0) * n

            def store(sl, total, q=q):
                acc[q, sl, cols] = total.astype(BF)

            add(
                n,
                store,
                lambda sl, base=base: x[shift(sl, base), cols],
                lambda sl, q=q: sibs[q, sl, cols],
            )
        tob = [
            push(acc.at[2 * j + 1, pl.ds(0, h), cols], r1b.at[j, :, cols], side)
            for j in range(span)
        ]
        toa = [
            [
                push(acc.at[2 * j + db, pl.ds(h, h), cols], r1a.at[j - 1, db, :, cols], along[j - 1])
                for db in range(2)
            ]
            for j in range(1, span)
        ]
        hop1.append((tob, toa))

    forward = []
    for i, (n, _) in enumerate(gathers):
        h = n // 2
        o = ag_out[i]
        b1, a2, b2, a1, s = own[i]
        b1.wait_recv()
        fa = [push(o.at[at(side, n, 0, h)], o.at[at(side, n, 0, h)], p) for p in along]
        fb = []
        for j in range(1, span):
            a2[j - 1].wait_recv()
            rows_in = at(behind[j - 1], n, h, h)
            fb.append(push(o.at[rows_in], o.at[rows_in], side))
        forward.append((fa, fb))

    hop2 = []
    for (i, cols), (tob, toa) in zip(parts, hop1):
        n = scatters[i][0] // rows
        h = n // 2
        _, acc, r1b, r1a, r2a, r2b = bufs[i]
        for copy in tob:
            copy.wait_recv()
        toa2 = []
        for j in range(1, span):

            def store(sl, total, j=j):
                acc[2 * j, sl, cols] = total.astype(BF)

            add(h, store, lambda sl, j=j: acc[2 * j, sl, cols], lambda sl, j=j: r1b[j, sl, cols])
            toa2.append(push(acc.at[2 * j, pl.ds(0, h), cols], r2a.at[j - 1, :, cols], along[j - 1]))
        for pair in toa:
            for copy in pair:
                copy.wait_recv()

        def store2(sl, total):
            acc[1, shift(sl, h), cols] = total.astype(BF)

        add(
            h,
            store2,
            lambda sl: acc[1, shift(sl, h), cols],
            *[lambda sl, j=j: r1a[j - 1, 1, sl, cols] for j in range(1, span)],
        )
        tob2 = push(acc.at[1, pl.ds(h, h), cols], r2b.at[:, cols], side)
        hop2.append((toa2, tob2))

    share = []
    for i, (n, _) in enumerate(gathers):
        o = ag_out[i]
        b1, a2, b2, a1, s = own[i]
        b2.wait_recv()
        blk = at(side, n, 0, n)
        share.append(push(o.at[blk], o.at[blk], sib))
        for j in range(1, span):
            a1[j - 1].wait_recv()
            blk = at(behind[j - 1], n, 0, n)
            share.append(push(o.at[blk], o.at[blk], sib))

    for (i, cols), (toa2, tob2) in zip(parts, hop2):
        n = scatters[i][0] // rows
        h = n // 2
        x, out = rs_in[i], rs_out[i]
        sibs, acc, r1b, r1a, r2a, r2b = bufs[i]
        for copy in toa2:
            copy.wait_recv()
        base = r * n

        def store1(sl, total):
            out[sl, cols] = total

        add(
            h,
            store1,
            lambda sl: x[shift(sl, base), cols],
            lambda sl: sibs[0, sl, cols],
            lambda sl: r1b[0, sl, cols],
            *[lambda sl, j=j: r2a[j - 1, sl, cols] for j in range(1, span)],
        )
        tob2.wait_recv()

        def store2(sl, total):
            out[shift(sl, h), cols] = total

        add(
            h,
            store2,
            lambda sl: x[shift(sl, base + h), cols],
            lambda sl: sibs[0, shift(sl, h), cols],
            *[lambda sl, j=j: r1a[j - 1, 0, sl, cols] for j in range(1, span)],
            lambda sl: r2b[sl, cols],
        )

    for i, (n, _) in enumerate(gathers):
        o = ag_out[i]
        fa, fb = forward[i]
        for j in range(1, span):
            fa[j - 1].wait_recv()
            fb[j - 1].wait_recv()
            blk = at(corner[j - 1], n, 0, n)
            share.append(push(o.at[blk], o.at[blk], sib))
    for group in own:
        group[4].wait_recv()
    for copy in share:
        copy.wait_recv()
    for copy in locals_:
        copy.wait()
    for copy in copies:
        copy.wait_send()


def exchange(rows, name, collective_id, gather, scatter):
    span = rows // 4
    gathers = [x.shape for x in gather]
    scatters = [x.shape for x in scatter]
    scratch = []
    for m, w in scatters:
        n = m // rows
        h = n // 2
        scratch += [
            pltpu.VMEM((2 * span, n, w), BF),
            pltpu.VMEM((2 * span, n, w), BF),
            pltpu.VMEM((span, h, w), BF),
            pltpu.VMEM((span - 1, 2, h, w), BF),
            pltpu.VMEM((span - 1, h, w), BF),
            pltpu.VMEM((h, w), BF),
        ]
    count = CHUNKS * len(scatters) * (6 * span - 2) + len(gathers) * (6 * span - 2)
    scratch += [
        pltpu.SemaphoreType.DMA((count,)),
        pltpu.SemaphoreType.DMA((count,)),
        pltpu.SemaphoreType.DMA((max(1, len(gathers)),)),
    ]
    moved = sum(m * w * 2 * rows for m, w in gathers) + sum(m * w * 2 for m, w in scatters)
    any_, vmem = pl.BlockSpec(memory_space=pl.ANY), pl.BlockSpec(memory_space=pltpu.VMEM)
    return pl.pallas_call(
        functools.partial(exchange_kernel, rows, gathers, scatters),
        out_shape=[jax.ShapeDtypeStruct((m * rows, w), BF) for m, w in gathers]
        + [jax.ShapeDtypeStruct((m // rows, w), F32) for m, w in scatters],
        in_specs=[any_] * len(gathers) + [vmem] * len(scatters),
        out_specs=[any_] * len(gathers) + [vmem] * len(scatters),
        scratch_shapes=scratch,
        compiler_params=pltpu.CompilerParams(
            collective_id=collective_id, has_side_effects=True, vmem_limit_bytes=48 * 1024 * 1024
        ),
        cost_estimate=pl.CostEstimate(flops=0, bytes_accessed=10 * moved, transcendentals=0),
        name=name,
    )(*gather, *scatter)


def body(tokens, cotangent, small_weight, expand_in, expand_out):
    rows = lax.axis_size("row")
    r = lax.axis_index("row")
    band = small_weight.shape[0] // rows
    mine = lax.dynamic_slice_in_dim(small_weight, r * band, band, 0)
    small_rows = lax.all_gather(mine, "col", axis=1, tiled=True)
    grad_part = dot(tokens, cotangent, 0, 0).astype(BF)
    out_panel, grad_grown = exchange(rows, "grad_grown", 1, [expand_out], [grad_part])
    grad_low = grad_grown.astype(BF)
    pair_part = dot(small_rows, out_panel, 1, 0).astype(BF)
    low_part = dot(expand_in, grad_low, 0, 0).astype(BF)
    pair, low = exchange(rows, "pair", 2, [pair_part], [low_part])
    low = low.astype(BF)
    grad_in = lax.psum_scatter(
        dot(grad_low, pair, 1, 1).astype(BF), "col", scatter_dimension=1, tiled=True
    ).astype(F32)
    grown = dot(expand_in, pair, 1, 0).astype(BF)
    out_part = dot(small_rows, low, 0, 0).astype(BF)
    grown_all, grad_out = exchange(rows, "grad_out", 3, [grown], [out_part])
    projected = dot(tokens, grown_all, 1, 0).astype(BF)
    return (projected, grad_grown, grad_in, grad_out)


def solution(mesh):
    in_specs = (P("row", None), P("row", "col"), P(None, "col"), P("row", None), P("row", "col"))
    out_specs = (P("row", "col"), P("row", "col"), P("row", "col"), P("row", "col"))
    return jax.shard_map(body, mesh=mesh, in_specs=in_specs, out_specs=out_specs, check_vma=False)
```

time: 546 us -> 332 us (0.61)
  waiting for transfers between devices: 424 us -> 0.04 us
  Pallas kernels: 0 us -> 225 us
  other arithmetic: 8.34 us -> 1.28 us
  matrix products: 75.6 us -> 69.4 us
    pallas_call x0 -> x3, Pallas kernels: none -> 225 us  [exchange(): pl.pallas_call(functools.partial(exchange_kernel, rows, gathers, scatters...]
    reduce_scatter x2 -> x0, waiting for transfers between devices: 148 us -> none  [the longest x1 77 us: body(): lax.psum_scatter(grad_part, 'row', scatter_dimension=0, tiled=True)]
    all_gather x3 -> x0, waiting for transfers between devices: 146 us -> none  [the longest x1 62.8 us: body(): grown_all = lax.all_gather(grown, 'row', axis=0, tiled=True)]
    unnamed x10 -> x3, waiting for transfers between devices: 90 us -> 0.03 us
    all_gather x1, waiting for transfers between devices: 40.6 us -> 0.01 us  [body(): small_rows = lax.all_gather(mine, 'col', axis=1, tiled=True)]
    dot_general x7, matrix products: 75.6 us -> 69.4 us  [dot(): lax.dot_general(a, b, (((ca,), (cb,)), ((), ())), preferred_element_type=...]
    convert_element_type x2 -> x0, other arithmetic: 5.92 us -> none  [the longest x1 3.13 us: body(): grad_grown = grad_sum.astype(F32)]
    unnamed x6 -> x27, local copies, waits for them, and re-layouts: 19.9 us -> 19 us
  transfers between devices with their start and end apart: 8 -> 2, of which waited for: 8 -> 0; matrix products, arithmetic and copies ran while one was open for 15% -> 18% of each run, Pallas kernels for 0% -> 53%
where the time goes in v2:
time: 332 us
  Pallas kernels  225 us (68%)
  matrix products  69.4 us (21%)
  local copies, waits for them, and re-layouts  21.1 us (6%)
  between operations  14.2 us (4%)
    pallas_call x3, Pallas kernels, exchange(): pl.pallas_call(functools.partial(exchange_kernel, rows, gathers, scatters...  225 us
    dot_general x7, matrix products, dot(): lax.dot_general(a, b, (((ca,), (cb,)), ((), ())), preferred_element_type=...  69.4 us
    unnamed x27, local copies, waits for them, and re-layouts  19 us
  transfers between devices with their start and end apart: 2, of which 0 were waited for; matrix products, arithmetic and copies ran while one was open for 18% of the time, Pallas kernels for 53%

profile of v2, /device:TPU:0, one launch (start us, length us, event | category | flops | bytes accessed | tf_op | source)
XLA Modules:
  0.0 331.6 jit_solution(8854158443726440294)
XLA Ops:
  7.2 0.0 copy-start
  7.2 0.0 all-gather.2.cloned.1.call-start
  7.2 2.1 constant_dynamic-slice_fusion
  9.4 0.0 all-gather.2.cloned.1.call-update
  9.4 0.0 reduce-scatter.4.cloned.1.call-start
  9.4 16.9 %convolution_convert_fusion.refs_1_ = bf16[5120,1024]{1,0:T(8,128)(2,1)} fusion(bf16[1024,5120]{1,0:T(8,128)(2,1)} %param.5, bf16[1024,1024]{1,0:T(8,128)(2,1)} %param.6), kind=kOutput, calls=%fused_computation | convolution fusion | flops 10742661120 | bytes 23068672 | tf_op jit(solution)/shard_map/dot_general | solution.py:17
  26.4 88.5 %grad_grown.1 = (bf16[4096,1024]{1,0:T(8,128)(2,1)}, f32[640,1024]{1,0:T(8,128)S(1)}) custom-call(bf16[512,1024]{1,0:T(8,128)(2,1)S(1)} %copy-done.6, bf16[5120,1024]{1,0:T(8,128)(2,1)} %convolution_convert_fusion.refs_1_), custom_call_target="tpu_custom_call" | custom-call | bytes 188743680 | tf_op jit(solution)/shard_map/grad_grown/pallas_call | solution.py:278
  114.8 1.5 copy-done.2
  116.3 6.1 %fusion.refs_1_ = bf16[2560,1024]{1,0:T(8,128)(2,1)} fusion(bf16[640,2560]{1,0:T(8,128)(2,1)S(1)} %copy-done, f32[640,1024]{1,0:T(8,128)S(1)} %get-tuple-element.29), kind=kOutput, calls=%fused_computation.3 | convolution fusion | flops 3358720000 | bytes 11141120 | tf_op jit(solution)/shard_map/dot_general | solution.py:17
  122.4 7.0 %convolution_convert_fusion.5.refs_0_ = bf16[320,1024]{1,0:T(8,128)(2,1)S(1)} fusion(bf16[320,4096]{1,0:T(8,128)(2,1)} %all-gather.2.cloned.1.call-done, bf16[4096,1024]{1,0:T(8,128)(2,1)} %get-tuple-element.10), kind=kOutput, calls=%fused_computation.8 | convolution fusion | flops 2684682240 | bytes 11665408 | tf_op jit(solution)/shard_map/dot_general | solution.py:17
  129.5 50.7 %pair.1 = (bf16[2560,1024]{1,0:T(8,128)(2,1)}, f32[320,1024]{1,0:T(8,128)S(1)}) custom-call(bf16[320,1024]{1,0:T(8,128)(2,1)S(1)} %convolution_convert_fusion.5.refs_0_, bf16[2560,1024]{1,0:T(8,128)(2,1)} %fusion.refs_1_), custom_call_target="tpu_custom_call" | custom-call | bytes 104857600 | tf_op jit(solution)/shard_map/pair/pallas_call | solution.py:278
  180.2 1.0 copy-done.7
  181.3 7.6 %convolution_convert_fusion.3 = bf16[640,2560]{1,0:T(8,128)(2,1)} fusion(bf16[2560,1024]{1,0:T(8,128)(2,1)} %get-tuple-element.12, f32[640,1024]{1,0:T(8,128)S(1)} %copy-done.3), kind=kOutput, calls=%fused_computation.4 | convolution fusion | flops 3357736960 | bytes 11141120 | tf_op jit(solution)/shard_map/dot_general | solution.py:17
  188.8 5.6 %copy.17 = bf16[640,2560]{0,1:T(8,128)(2,1)} copy(bf16[640,2560]{1,0:T(8,128)(2,1)} %convolution_convert_fusion.3) | data formatting | bytes 6553600
  194.4 0.0 reduce-scatter.4.cloned.1.call-update
  194.5 10.2 %convolution_convert_fusion.1.refs_1_ = bf16[4096,1024]{1,0:T(8,128)(2,1)} fusion(bf16[320,4096]{1,0:T(8,128)(2,1)} %all-gather.2.cloned.1.call-done, f32[320,1024]{1,0:T(8,128)} %copy-done.7), kind=kOutput, calls=%fused_computation.1 | convolution fusion | flops 2688876544 | bytes 12320768 | tf_op jit(solution)/shard_map/dot_general | solution.py:17
  204.7 6.2 %fusion.1.refs_0_ = bf16[640,1024]{1,0:T(8,128)(2,1)S(1)} fusion(bf16[640,2560]{1,0:T(8,128)(2,1)S(1)} %copy-done, bf16[2560,1024]{1,0:T(8,128)(2,1)} %get-tuple-element.12), kind=kOutput, calls=%fused_computation.7 | convolution fusion | flops 3356098560 | bytes 9830400 | tf_op jit(solution)/shard_map/dot_general | solution.py:17
  210.8 86.3 %grad_out.1 = (bf16[5120,1024]{1,0:T(8,128)(2,1)}, f32[512,1024]{1,0:T(8,128)S(1)}) custom-call(bf16[640,1024]{1,0:T(8,128)(2,1)S(1)} %fusion.1.refs_0_, bf16[4096,1024]{1,0:T(8,128)(2,1)} %convolution_convert_fusion.1.refs_1_), custom_call_target="tpu_custom_call" | custom-call | bytes 188743680 | tf_op jit(solution)/shard_map/grad_out/pallas_call | solution.py:278
  297.2 15.4 %convert_bitcast_fusion = bf16[1024,1024]{0,1:T(8,128)(2,1)} fusion(bf16[5120,1024]{1,0:T(8,128)(2,1)} %get-tuple-element.14, bf16[1024,5120]{1,0:T(8,128)(2,1)S(1)} %bitcast.22), kind=kOutput, calls=%fused_computation.5 | convolution fusion | flops 10738466816 | bytes 23068672 | tf_op jit(solution)/shard_map/dot_general | solution.py:17
  312.7 3.9 %copy.14 = bf16[1024,1024]{1,0:T(8,128)(2,1)} copy(bf16[1024,1024]{0,1:T(8,128)(2,1)} %convert_bitcast_fusion) | data formatting | bytes 4194304
  316.6 1.8 copy.18
  318.4 1.3 convert_element_type.49
  319.7 3.7 %copy.21 = f32[640,1024]{1,0:T(8,128)} copy(f32[640,1024]{1,0:T(8,128)} %copy-done.2) | data formatting | bytes 5242880
  323.4 1.3 copy.22
  (22 shorter events, 0.0 us)
Async XLA Ops:
  7.2 109.2 %copy-start = (bf16[640,2560]{1,0:T(8,128)(2,1)S(1)}, bf16[640,2560]{1,0:T(8,128)(2,1)}, u32[]{:S(2)}) copy-start(bf16[640,2560]{1,0:T(8,128)(2,1)} %param.8) | copy-start | bytes 9830404
  7.2 115.3 %all-gather.2.cloned.1.call-start = ((), (), s32[]{:S(2)}) async-start(), calls=%async_computation.1 | async-start | bytes 3276800 | tf_op jit(solution)/shard_map/all_gather | solution.py:298
  9.4 307.2 %reduce-scatter.4.cloned.1.call-start = ((), (), s32[]{:S(2)}) async-start(), calls=%async_computation.2 | async-start | bytes 4096000
  9.4 16.9 %copy-start.6 = (bf16[512,1024]{1,0:T(8,128)(2,1)S(1)}, bf16[512,1024]{1,0:T(8,128)(2,1)}, u32[]{:S(2)}) copy-start(bf16[512,1024]{1,0:T(8,128)(2,1)} %refs_0_.1) | copy-start | bytes 3145732
  114.8 1.5 copy-start.2
  129.5 51.8 %copy-start.3 = (f32[640,1024]{1,0:T(8,128)S(1)}, f32[640,1024]{1,0:T(8,128)}, u32[]{:S(2)}) copy-start(f32[640,1024]{1,0:T(8,128)} %copy-done.2) | copy-start | bytes 7864324
  180.2 1.1 copy-start.7
  194.5 102.7 %slice-start = ((s8[10485760]{0:T(1024)(128)(4,1)}), s8[4194304]{0:T(1024)(128)(4,1)S(1)}, s32[]{:S(2)}) async-start(s8[10485760]{0:T(1024)(128)(4,1)} %bitcast.21), calls=%async_computation.3 | async-start | bytes 8388608
  204.6 92.5 %slice-start.1 = ((s8[10485760]{0:T(1024)(128)(4,1)}), s8[4194304]{0:T(1024)(128)(4,1)S(1)}, s32[]{:S(2)}) async-start(s8[10485760]{0:T(1024)(128)(4,1)} %bitcast.21), calls=%async_computation.4 | async-start | bytes 8388608
  204.7 92.6 %slice-start.2 = ((s8[10485760]{0:T(1024)(128)(4,1)}), s8[2097152]{0:T(1024)(128)(4,1)S(1)}, s32[]{:S(2)}) async-start(s8[10485760]{0:T(1024)(128)(4,1)} %bitcast.21), calls=%async_computation.5 | async-start | bytes 4194304
  297.2 15.5 %copy-start.4 = (f32[512,1024]{1,0:T(8,128)}, f32[512,1024]{1,0:T(8,128)S(1)}, u32[]{:S(2)}) copy-start(f32[512,1024]{1,0:T(8,128)S(1)} %get-tuple-element.31) | copy-start | bytes 6291460
  318.4 5.0 %copy-start.5 = (f32[512,1024]{1,0:T(8,128)S(1)}, f32[512,1024]{1,0:T(8,128)}, u32[]{:S(2)}) copy-start(f32[512,1024]{1,0:T(8,128)} %copy-done.4) | copy-start | bytes 6291460
  319.7 5.0 %copy-start.1 = (bf16[640,2560]{1,0:T(8,128)(2,1)S(1)}, bf16[640,2560]{1,0:T(8,128)(2,1)}, u32[]{:S(2)}) copy-start(bf16[640,2560]{1,0:T(8,128)(2,1)} %param.8) | copy-start | bytes 9830404
Sparse Core Ops, SparseCore 0:
  10.2 57.4 all-gather.1
  194.6 62.6 reduce-scatter.3

commit v3 on v2

--- a/solution.py
+++ b/solution.py
@@ -17,11 +17,30 @@
     return lax.dot_general(a, b, (((ca,), (cb,)), ((), ())), preferred_element_type=F32)
 
 
-def exchange_kernel(rows, gathers, scatters, *refs):
+def exchange_kernel(rows, gathers, scatters, make, use, *refs):
     na, nr = len(gathers), len(scatters)
-    ag_in, rs_in = refs[:na], refs[na : na + nr]
-    ag_out, rs_out = refs[na + nr : 2 * na + nr], refs[2 * na + nr : 2 * na + 2 * nr]
-    scratch = refs[2 * na + 2 * nr :]
+    refs = list(refs)
+
+    def take(count):
+        taken, refs[:] = refs[:count], refs[count:]
+        return taken
+
+    ag_in = take(na)
+    rs_in = take(0 if make else nr)
+    tokens = take(1)[0] if make or use else None
+    cotangent = take(1)[0] if make else None
+    ag_out = take(0 if use else na)
+    rs_out = take(nr)
+    product = take(1)[0] if use else None
+    if make or use:
+        held, held_sem = take(2)
+    if make:
+        held_cot, terms = take(2)
+        rs_in = [terms]
+    if use:
+        whole, total = take(2)
+        ag_out = [whole]
+    scratch = refs
     bufs = [scratch[6 * i : 6 * i + 6] for i in range(nr)]
     send_sems, recv_sems, local_sems = scratch[6 * nr :]
     span = rows // 4
@@ -62,24 +81,68 @@
     def at(block, n, start, size):
         return pl.ds(pl.multiple_of(block * n + start, 16), size)
 
+    if make or use:
+        fetch = pltpu.make_async_copy(tokens, held, held_sem.at[0])
+        fetch.start()
+    if make:
+        fetch_cot = pltpu.make_async_copy(cotangent, held_cot, held_sem.at[1])
+        fetch_cot.start()
     parts = []
     for i, (_, w) in enumerate(scatters):
         for c in range(CHUNKS):
             parts.append((i, pl.ds(c * (w // CHUNKS), w // CHUNKS)))
 
-    first = []
-    for i, cols in parts:
-        n = scatters[i][0] // rows
-        first.append(
-            [
-                push(
-                    rs_in[i].at[at(index(q // 2, q % 2, 1), n, 0, n), cols],
-                    bufs[i][0].at[q, :, cols],
-                    sib,
-                )
-                for q in list(range(1, 2 * span)) + [0]
-            ]
-        )
+    def add(size, store, *loads):
+        def step(t):
+            sl = pl.ds(pl.multiple_of(t * TILE, TILE), TILE)
+            total = loads[0](sl).astype(F32)
+            for load in loads[1:]:
+                total = total + load(sl).astype(F32)
+            store(sl, total)
+
+        pl.loop(0, size // TILE)(step)
+
+    def shift(sl, start):
+        return pl.ds(pl.multiple_of(sl.start + start, TILE), TILE)
+
+    def multiply(q):
+        if not use:
+            return
+        n = gathers[0][0]
+        start = pl.multiple_of(index(q // 2, q % 2, 0) // 2 * 2 * n, 128)
+        height = min(256, tokens.shape[0])
+
+        def tile(t):
+            sl = pl.ds(pl.multiple_of(t * height, TILE), height)
+            term = dot(held[sl, pl.ds(start, 2 * n)], whole[pl.ds(start, 2 * n), :], 1, 0)
+            if q == 0:
+                total[sl, :] = term
+            elif q == 2 * span - 1:
+                product[sl, :] = (total[sl, :] + term).astype(BF)
+            else:
+                total[sl, :] += term
+
+        pl.loop(0, tokens.shape[0] // height)(tile)
+
+    def send_terms():
+        first = []
+        for i, cols in parts:
+            n = scatters[i][0] // rows
+            first.append(
+                [
+                    push(
+                        rs_in[i].at[at(index(q // 2, q % 2, 1), n, 0, n), cols],
+                        bufs[i][0].at[q, :, cols],
+                        sib,
+                    )
+                    for q in list(range(1, 2 * span)) + [0]
+                ]
+            )
+
+        return first
+
+    if not make:
+        first = send_terms()
 
     locals_ = []
     own = []
@@ -96,65 +159,90 @@
         s = push(x, o.at[at(r, n, 0, n)], sib)
         own.append((b1, a2, b2, a1, s))
 
-    def add(size, store, *loads):
-        def step(t):
-            sl = pl.ds(pl.multiple_of(t * TILE, TILE), TILE)
-            total = loads[0](sl).astype(F32)
-            for load in loads[1:]:
-                total = total + load(sl).astype(F32)
-            store(sl, total)
-
-        pl.loop(0, size // TILE)(step)
-
-    def shift(sl, start):
-        return pl.ds(pl.multiple_of(sl.start + start, TILE), TILE)
-
-    hop1 = []
-    for (i, cols), arrivals in zip(parts, first):
-        n = scatters[i][0] // rows
-        h = n // 2
-        x = rs_in[i]
-        sibs, acc, r1b, r1a, _, _ = bufs[i]
-        for copy in arrivals:
-            copy.wait_recv()
-        for q in range(1, 2 * span):
-            base = index(q // 2, q % 2, 0) * n
-
-            def store(sl, total, q=q):
-                acc[q, sl, cols] = total.astype(BF)
-
-            add(
-                n,
-                store,
-                lambda sl, base=base: x[shift(sl, base), cols],
-                lambda sl, q=q: sibs[q, sl, cols],
-            )
-        tob = [
-            push(acc.at[2 * j + 1, pl.ds(0, h), cols], r1b.at[j, :, cols], side)
-            for j in range(span)
-        ]
-        toa = [
-            [
-                push(acc.at[2 * j + db, pl.ds(h, h), cols], r1a.at[j - 1, db, :, cols], along[j - 1])
-                for db in range(2)
+    if make:
+        n = scatters[0][0] // rows
+        width = 2 * n if n % 128 else n
+        fetch.wait()
+        fetch_cot.wait()
+        first = [[] for _ in parts]
+        for q in list(range(1, 2 * span)) + [0]:
+            chip = index(q // 2, q % 2, 0) // 2
+
+            def tile(t):
+                start = pl.multiple_of(chip * 2 * n + t * width, 128)
+                terms[pl.ds(start, width), :] = dot(
+                    held[:, pl.ds(start, width)], held_cot[...], 0, 0
+                ).astype(BF)
+
+            pl.loop(0, 2 * n // width)(tile)
+            for (_, cols), group in zip(parts, first):
+                rows_out = at(index(q // 2, q % 2, 1), n, 0, n)
+                group.append(push(terms.at[rows_out, cols], bufs[0][0].at[q, :, cols], sib))
+
+    def hop_one():
+        hop1 = []
+        for (i, cols), arrivals in zip(parts, first):
+            n = scatters[i][0] // rows
+            h = n // 2
+            x = rs_in[i]
+            sibs, acc, r1b, r1a, _, _ = bufs[i]
+            for copy in arrivals:
+                copy.wait_recv()
+            for q in range(1, 2 * span):
+                base = index(q // 2, q % 2, 0) * n
+
+                def store(sl, total, q=q):
+                    acc[q, sl, cols] = total.astype(BF)
+
+                add(
+                    n,
+                    store,
+                    lambda sl, base=base: x[shift(sl, base), cols],
+                    lambda sl, q=q: sibs[q, sl, cols],
+                )
+            tob = [
+                push(acc.at[2 * j + 1, pl.ds(0, h), cols], r1b.at[j, :, cols], side)
+                for j in range(span)
             ]
-            for j in range(1, span)
-        ]
-        hop1.append((tob, toa))
-
-    forward = []
-    for i, (n, _) in enumerate(gathers):
-        h = n // 2
-        o = ag_out[i]
-        b1, a2, b2, a1, s = own[i]
-        b1.wait_recv()
-        fa = [push(o.at[at(side, n, 0, h)], o.at[at(side, n, 0, h)], p) for p in along]
-        fb = []
-        for j in range(1, span):
-            a2[j - 1].wait_recv()
-            rows_in = at(behind[j - 1], n, h, h)
-            fb.append(push(o.at[rows_in], o.at[rows_in], side))
-        forward.append((fa, fb))
+            toa = [
+                [
+                    push(acc.at[2 * j + db, pl.ds(h, h), cols], r1a.at[j - 1, db, :, cols], along[j - 1])
+                    for db in range(2)
+                ]
+                for j in range(1, span)
+            ]
+            hop1.append((tob, toa))
+
+        return hop1
+
+    def hop_gather():
+        forward = []
+        for i, (n, _) in enumerate(gathers):
+            h = n // 2
+            o = ag_out[i]
+            b1, a2, b2, a1, s = own[i]
+            b1.wait_recv()
+            fa = [push(o.at[at(side, n, 0, h)], o.at[at(side, n, 0, h)], p) for p in along]
+            fb = []
+            for j in range(1, span):
+                a2[j - 1].wait_recv()
+                rows_in = at(behind[j - 1], n, h, h)
+                fb.append(push(o.at[rows_in], o.at[rows_in], side))
+            forward.append((fa, fb))
+
+        return forward
+
+    if make:
+        forward = hop_gather()
+        hop1 = hop_one()
+    else:
+        hop1 = hop_one()
+        forward = hop_gather()
+    if use:
+        fetch.wait()
+        own[0][4].wait_recv()
+        locals_[0].wait()
+        multiply(0)
 
     hop2 = []
     for (i, cols), (tob, toa) in zip(parts, hop1):
@@ -199,6 +287,13 @@
             blk = at(behind[j - 1], n, 0, n)
             share.append(push(o.at[blk], o.at[blk], sib))
 
+    shared = list(share)
+    if use:
+        for copy in shared:
+            copy.wait_recv()
+        for q in [1] + [2 * j for j in range(1, span)]:
+            multiply(q)
+
     for (i, cols), (toa2, tob2) in zip(parts, hop2):
         n = scatters[i][0] // rows
         h = n // 2
@@ -241,21 +336,37 @@
             fb[j - 1].wait_recv()
             blk = at(corner[j - 1], n, 0, n)
             share.append(push(o.at[blk], o.at[blk], sib))
-    for group in own:
-        group[4].wait_recv()
-    for copy in share:
+    if not use:
+        for group in own:
+            group[4].wait_recv()
+        for copy in shared:
+            copy.wait_recv()
+        for copy in locals_:
+            copy.wait()
+    for copy in share[len(shared) :]:
         copy.wait_recv()
-    for copy in locals_:
-        copy.wait()
+    for j in range(1, span):
+        multiply(2 * j + 1)
     for copy in copies:
         copy.wait_send()
 
 
-def exchange(rows, name, collective_id, gather, scatter):
+def exchange(rows, name, collective_id, gather, scatter, make=None, use=None):
     span = rows // 4
     gathers = [x.shape for x in gather]
-    scatters = [x.shape for x in scatter]
+    scatters = [(make[0].shape[1], make[1].shape[1])] if make else [x.shape for x in scatter]
+    extra = list(make) if make else [use] if use is not None else []
     scratch = []
+    if extra:
+        scratch += [pltpu.VMEM(extra[0].shape, BF), pltpu.SemaphoreType.DMA((2,))]
+    if make:
+        scratch += [pltpu.VMEM(make[1].shape, BF), pltpu.VMEM(scatters[0], BF)]
+    products = []
+    if use is not None:
+        (n, w), m = gathers[0], use.shape[0]
+        scratch += [pltpu.VMEM((rows * n, w), BF), pltpu.VMEM((m, w), F32)]
+        products = [jax.ShapeDtypeStruct((m, w), BF)]
+    kept = 0 if use is not None else len(gathers)
     for m, w in scatters:
         n = m // rows
         h = n // 2
@@ -276,18 +387,21 @@
     moved = sum(m * w * 2 * rows for m, w in gathers) + sum(m * w * 2 for m, w in scatters)
     any_, vmem = pl.BlockSpec(memory_space=pl.ANY), pl.BlockSpec(memory_space=pltpu.VMEM)
     return pl.pallas_call(
-        functools.partial(exchange_kernel, rows, gathers, scatters),
-        out_shape=[jax.ShapeDtypeStruct((m * rows, w), BF) for m, w in gathers]
-        + [jax.ShapeDtypeStruct((m // rows, w), F32) for m, w in scatters],
-        in_specs=[any_] * len(gathers) + [vmem] * len(scatters),
-        out_specs=[any_] * len(gathers) + [vmem] * len(scatters),
+        functools.partial(
+            exchange_kernel, rows, gathers, scatters, make is not None, use is not None
+        ),
+        out_shape=[jax.ShapeDtypeStruct((m * rows, w), BF) for m, w in gathers[:kept]]
+        + [jax.ShapeDtypeStruct((m // rows, w), F32) for m, w in scatters]
+        + products,
+        in_specs=[any_] * len(gathers) + [vmem] * len(scatter) + [any_] * len(extra),
+        out_specs=[any_] * kept + [vmem] * (len(scatters) + len(products)),
         scratch_shapes=scratch,
         compiler_params=pltpu.CompilerParams(
-            collective_id=collective_id, has_side_effects=True, vmem_limit_bytes=48 * 1024 * 1024
+            collective_id=collective_id, has_side_effects=True, vmem_limit_bytes=58 * 1024 * 1024
         ),
         cost_estimate=pl.CostEstimate(flops=0, bytes_accessed=10 * moved, transcendentals=0),
         name=name,
-    )(*gather, *scatter)
+    )(*gather, *scatter, *extra)
 
 
 def body(tokens, cotangent, small_weight, expand_in, expand_out):
@@ -296,8 +410,9 @@
     band = small_weight.shape[0] // rows
     mine = lax.dynamic_slice_in_dim(small_weight, r * band, band, 0)
     small_rows = lax.all_gather(mine, "col", axis=1, tiled=True)
-    grad_part = dot(tokens, cotangent, 0, 0).astype(BF)
-    out_panel, grad_grown = exchange(rows, "grad_grown", 1, [expand_out], [grad_part])
+    out_panel, grad_grown = exchange(
+        rows, "grad_grown", 1, [expand_out], [], make=(tokens, cotangent)
+    )
     grad_low = grad_grown.astype(BF)
     pair_part = dot(small_rows, out_panel, 1, 0).astype(BF)
     low_part = dot(expand_in, grad_low, 0, 0).astype(BF)
@@ -308,8 +423,7 @@
     ).astype(F32)
     grown = dot(expand_in, pair, 1, 0).astype(BF)
     out_part = dot(small_rows, low, 0, 0).astype(BF)
-    grown_all, grad_out = exchange(rows, "grad_out", 3, [grown], [out_part])
-    projected = dot(tokens, grown_all, 1, 0).astype(BF)
+    grad_out, projected = exchange(rows, "grad_out", 3, [grown], [out_part], use=tokens)
     return (projected, grad_grown, grad_in, grad_out)
 
 

time: 332 us -> 304 us (0.916)
  matrix products: 69.4 us -> 40.2 us
  Pallas kernels: 225 us -> 230 us
  local copies, waits for them, and re-layouts: 21.1 us -> 16.9 us
    dot_general x7 -> x5, matrix products: 69.4 us -> 40.2 us  [dot(): lax.dot_general(a, b, (((ca,), (cb,)), ((), ())), preferred_element_type=...]
    unnamed x27 -> x13, local copies, waits for them, and re-layouts: 19 us -> 14.8 us
    pallas_call x3, Pallas kernels: 225 us -> 230 us  [exchange(): pl.pallas_call(functools.partial(exchange_kernel, rows, gathers, scatters...]
  transfers between devices with their start and end apart: 2 -> 2, of which waited for: 0 -> 0; matrix products, arithmetic and copies ran while one was open for 18% -> 8% of each run, Pallas kernels for 53% -> 59%
where the time goes in v3:
time: 304 us; the launch traced here: 303 us
  Pallas kernels  230 us (76%)
  matrix products  40.2 us (13%)
  local copies, waits for them, and re-layouts  16.9 us (6%)
  between operations  14.1 us (5%)
    pallas_call x3, Pallas kernels, exchange(): pl.pallas_call(functools.partial(exchange_kernel, rows, gathers, scatters...  230 us
    dot_general x5, matrix products, dot(): lax.dot_general(a, b, (((ca,), (cb,)), ((), ())), preferred_element_type=...  40.2 us
    unnamed x13, local copies, waits for them, and re-layouts  14.8 us
  transfers between devices with their start and end apart: 2, of which 0 were waited for; matrix products, arithmetic and copies ran while one was open for 8% of the time, Pallas kernels for 59%

profile of v3, /device:TPU:0, one launch (start us, length us, event | category | flops | bytes accessed | tf_op | source)
XLA Modules:
  0.0 303.4 jit_solution(1927296560278662304)
XLA Ops:
  7.2 0.0 copy-start
  7.2 0.0 all-gather.2.cloned.1.call-start
  7.2 2.1 constant_dynamic-slice_fusion
  9.4 0.0 all-gather.2.cloned.1.call-update
  9.4 0.0 reduce-scatter.4.cloned.1.call-start
  9.4 86.2 %grad_grown.1 = (bf16[4096,1024]{1,0:T(8,128)(2,1)}, f32[640,1024]{1,0:T(8,128)}) custom-call(bf16[512,1024]{1,0:T(8,128)(2,1)} %refs_0_.1, bf16[1024,5120]{1,0:T(8,128)(2,1)} %refs_2_.3, bf16[1024,1024]{1,0:T(8,128)(2,1)} %refs_2_.2), custom_call_target="tpu_custom_call" | custom-call | bytes 188743680 | tf_op jit(solution)/shard_map/grad_grown/pallas_call | solution.py:389
  95.7 0.0 copy-done
  95.7 7.8 %fusion.refs_1_ = bf16[2560,1024]{1,0:T(8,128)(2,1)} fusion(bf16[640,2560]{1,0:T(8,128)(2,1)S(1)} %copy-done, f32[640,1024]{1,0:T(8,128)} %get-tuple-element.21), kind=kOutput, calls=%fused_computation.2 | convolution fusion | flops 3358720000 | bytes 11141120 | tf_op jit(solution)/shard_map/dot_general | solution.py:17
  103.5 7.9 %convolution_convert_fusion.4.refs_0_ = bf16[320,1024]{1,0:T(8,128)(2,1)} fusion(bf16[320,4096]{1,0:T(8,128)(2,1)} %all-gather.2.cloned.1.call-done, bf16[4096,1024]{1,0:T(8,128)(2,1)} %get-tuple-element.10), kind=kOutput, calls=%fused_computation.6 | convolution fusion | flops 2684682240 | bytes 11665408 | tf_op jit(solution)/shard_map/dot_general | solution.py:17
  111.4 52.0 %pair.1 = (bf16[2560,1024]{1,0:T(8,128)(2,1)}, f32[320,1024]{1,0:T(8,128)}) custom-call(bf16[320,1024]{1,0:T(8,128)(2,1)} %convolution_convert_fusion.4.refs_0_, bf16[2560,1024]{1,0:T(8,128)(2,1)} %fusion.refs_1_), custom_call_target="tpu_custom_call" | custom-call | bytes 104857600 | tf_op jit(solution)/shard_map/pair/pallas_call | solution.py:389
  163.3 0.0 copy-done.1
  163.4 7.5 %convolution_convert_fusion.2 = bf16[640,2560]{1,0:T(8,128)(2,1)} fusion(bf16[2560,1024]{1,0:T(8,128)(2,1)} %get-tuple-element.12, f32[640,1024]{1,0:T(8,128)S(1)} %copy-done.1), kind=kOutput, calls=%fused_computation.3 | convolution fusion | flops 3357736960 | bytes 11141120 | tf_op jit(solution)/shard_map/dot_general | solution.py:17
  170.8 5.7 %copy.15 = bf16[640,2560]{0,1:T(8,128)(2,1)} copy(bf16[640,2560]{1,0:T(8,128)(2,1)} %convolution_convert_fusion.2) | data formatting | bytes 6553600
  176.5 0.0 reduce-scatter.4.cloned.1.call-update
  176.5 9.9 %convolution_convert_fusion.refs_1_ = bf16[4096,1024]{1,0:T(8,128)(2,1)} fusion(bf16[320,4096]{1,0:T(8,128)(2,1)} %all-gather.2.cloned.1.call-done, f32[320,1024]{1,0:T(8,128)} %get-tuple-element.13), kind=kOutput, calls=%fused_computation | convolution fusion | flops 2688876544 | bytes 12320768 | tf_op jit(solution)/shard_map/dot_general | solution.py:17
  186.5 7.1 %fusion.1.refs_0_ = bf16[640,1024]{1,0:T(8,128)(2,1)} fusion(bf16[640,2560]{1,0:T(8,128)(2,1)S(1)} %copy-done, bf16[2560,1024]{1,0:T(8,128)(2,1)} %get-tuple-element.12), kind=kOutput, calls=%fused_computation.5 | convolution fusion | flops 3356098560 | bytes 9830400 | tf_op jit(solution)/shard_map/dot_general | solution.py:17
  193.6 91.3 %grad_out.1 = (f32[512,1024]{1,0:T(8,128)}, bf16[1024,1024]{1,0:T(8,128)(2,1)}) custom-call(bf16[640,1024]{1,0:T(8,128)(2,1)} %fusion.1.refs_0_, bf16[4096,1024]{1,0:T(8,128)(2,1)} %convolution_convert_fusion.refs_1_, bf16[1024,5120]{1,0:T(8,128)(2,1)} %refs_2_.3), custom_call_target="tpu_custom_call" | custom-call | bytes 188743680 | tf_op jit(solution)/shard_map/grad_out/pallas_call | solution.py:389
  284.9 0.0 reduce-scatter.4.cloned.1.call-done
  284.9 2.2 copy.16
  287.1 2.6 convert_element_type.37
  289.7 3.1 %copy.20 = bf16[1024,1024]{1,0:T(8,128)(2,1)} copy(bf16[1024,1024]{1,0:T(8,128)(2,1)} %get-tuple-element.20) | data formatting | bytes 4194304
  292.7 1.5 copy.21
  294.2 1.0 copy-done.3
  295.3 1.3 copy.22
  (5 shorter events, 0.0 us)
Async XLA Ops:
  7.2 88.5 %copy-start = (bf16[640,2560]{1,0:T(8,128)(2,1)S(1)}, bf16[640,2560]{1,0:T(8,128)(2,1)}, u32[]{:S(2)}) copy-start(bf16[640,2560]{1,0:T(8,128)(2,1)} %param.8) | copy-start | bytes 9830404
  7.2 96.3 %all-gather.2.cloned.1.call-start = ((), (), s32[]{:S(2)}) async-start(), calls=%async_computation.1 | async-start | bytes 3276800 | tf_op jit(solution)/shard_map/all_gather | solution.py:412
  9.4 275.5 %reduce-scatter.4.cloned.1.call-start = ((), (), s32[]{:S(2)}) async-start(), calls=%async_computation.2 | async-start | bytes 4096000
  111.4 52.0 %copy-start.1 = (f32[640,1024]{1,0:T(8,128)S(1)}, f32[640,1024]{1,0:T(8,128)}, u32[]{:S(2)}) copy-start(f32[640,1024]{1,0:T(8,128)} %get-tuple-element.21) | copy-start | bytes 7864324
  287.1 5.7 %copy-start.2 = (f32[640,1024]{1,0:T(8,128)S(1)}, f32[640,1024]{1,0:T(8,128)}, u32[]{:S(2)}) copy-start(f32[640,1024]{1,0:T(8,128)} %get-tuple-element.21) | copy-start | bytes 7864324
  292.7 2.5 copy-start.3
Sparse Core Ops, SparseCore 0:
  10.2 57.4 all-gather.1
  176.6 62.6 reduce-scatter.3
